TPU v7x, 512 devices: a whole 4x4x16 slice. The times are simulated.
512 devices in a mesh: seq: 64 (over x, z), head: 8 (over y, core).
Axes of the slice: x: 4, y: 4, z: 16, core: 2. Of those that a mesh axis runs over, the one named last changes fastest.
Arguments:
- queries: bfloat16 [256, 8192], P('seq', 'head'), may hold values from -8 to 8
- doc_kv: bfloat16 [2, 131072, 1024], P(None, 'seq', 'head'), may hold values from -4 to 4
- leaf_kv: bfloat16 [2, 65536, 1024], P(None, 'seq', 'head'), may hold values from -4 to 4
- suffix_kv: bfloat16 [2, 256, 512, 1024], P(None, 'seq', None, 'head'), may hold values from -4 to 4
- suffix_len: int32 [256], P('seq'), may hold values from 1 to 512, as said below
- parent: int32 [64], replicated, may hold values from 0 to 15, as said below
- row_leaf: int32 [256], replicated, may hold values from 0 to 63, as said below
- out_weight: bfloat16 [8192, 8192], P('head', 'seq'), may hold values from -0.25 to 0.25
Outputs:
- layer_out: bfloat16 [256, 8192], P('head', 'seq')
Inputs may be any that keep to these rules, and one draw needn't show every extreme that they name: Every document is the parent of exactly 4 second-level nodes. `row_leaf`: at most 12 rows have the same second-level node; every node of one document has exactly 12. `suffix_len`: some row has all 512 suffix tokens live.
All inputs are finite; a program needn't handle non-finite values.
Results may differ from a plain program's by a relative error of at most 0.0052.
Values may be sent and summed in bfloat16 or wider, within the bound.
A program may use at most 64 MiB of HBM per device.

v0:
```python
import math

import jax
import jax.numpy as jnp
from jax import lax
from jax.sharding import PartitionSpec as P

QH = 64
KVH = 8
HD = 128
NODES1 = 16


NEG_FILL = -1e30


def block_size(row_count):
    return math.gcd(row_count, 64)


def blocked(tensors):
    row_count = tensors[0].shape[0]
    stride = block_size(row_count)
    return tuple(
        (element.reshape((row_count // stride, stride) + element.shape[1:]) for element in tensors)
    )


def masked_scores(query_block, key_rows, usable):
    scaling = query_block.shape[-1] ** (-0.5)
    scores = (
        jnp.einsum("bkgh,tkh->bkgt", query_block, key_rows, preferred_element_type=jnp.float32)
        * scaling
    )
    return jnp.where(usable[:, None, None, None], scores, NEG_FILL)


def segment_peak(query_rows, usable, key_rows):

    def per_block(blocks):
        return jnp.max(masked_scores(blocks[0], key_rows, blocks[1]), axis=-1)

    result = lax.map(per_block, blocked((query_rows, usable)))
    return result.reshape(query_rows.shape[:3])


def segment_terms(query_rows, usable, row_peak, key_rows, value_rows):

    def per_block(blocks):
        scores = masked_scores(blocks[0], key_rows, blocks[1])
        weights = jnp.exp(scores - blocks[2][..., None])
        rounded = weights.astype(jnp.bfloat16)
        accum = jnp.einsum(
            "bkgt,tkh->bkgh", rounded, value_rows, preferred_element_type=jnp.float32
        )
        return (accum, jnp.sum(weights, axis=-1))

    accum, totals = lax.map(per_block, blocked((query_rows, usable, row_peak)))
    return (accum.reshape(query_rows.shape), totals.reshape(query_rows.shape[:3]))


def normalized(accum, totals, head_count):
    row_count = accum.shape[0]
    shaped = accum.reshape(row_count, head_count, -1) / totals[..., None]
    return shaped.reshape(row_count, -1).astype(jnp.bfloat16)


def per_device(queries, doc_kv, leaf_kv, suffix_kv, suffix_len, parent, row_leaf, out_weight):
    seq_count = lax.axis_size("seq")
    position = lax.axis_index("seq")
    rows_here = queries.shape[0]
    rows_all = rows_here * seq_count
    heads_here = doc_kv.shape[2] // HD
    group_size = QH // KVH
    head_count = heads_here * group_size

    def split_heads(matrix):
        return matrix.reshape(matrix.shape[0], heads_here, group_size, HD)

    doc_keys = doc_kv[0].reshape(-1, heads_here, HD)
    doc_values = doc_kv[1].reshape(-1, heads_here, HD)
    leaf_keys = leaf_kv[0].reshape(-1, heads_here, HD)
    leaf_values = leaf_kv[1].reshape(-1, heads_here, HD)
    suffix_keys = suffix_kv[0].reshape(rows_here, -1, heads_here, HD)
    suffix_values = suffix_kv[1].reshape(rows_here, -1, heads_here, HD)
    everyone = split_heads(lax.all_gather(queries, "seq", axis=0, tiled=True))
    own_queries = split_heads(queries)
    own_start = position * rows_here
    leaf_ids = jnp.arange(parent.shape[0], dtype=jnp.int32)
    row_doc = jnp.sum(jnp.where(row_leaf[:, None] == leaf_ids[None, :], parent[None, :], 0), axis=1)
    doc_member = row_doc == position // (seq_count // NODES1)
    leaf_member = row_leaf == position
    suffix_usable = jnp.arange(suffix_keys.shape[1], dtype=jnp.int32)[None, :] < suffix_len[:, None]
    suffix_scores = jnp.einsum(
        "rkgh,rtkh->rkgt", own_queries, suffix_keys, preferred_element_type=jnp.float32
    ) * HD ** (-0.5)
    suffix_scores = jnp.where(suffix_usable[:, None, None, :], suffix_scores, NEG_FILL)
    doc_peak = segment_peak(everyone, doc_member, doc_keys)
    leaf_peak = segment_peak(everyone, leaf_member, leaf_keys)
    local_peak = jnp.maximum(doc_peak, leaf_peak)
    own_peak = lax.dynamic_slice_in_dim(local_peak, own_start, rows_here, 0)
    local_peak = lax.dynamic_update_slice_in_dim(
        local_peak, jnp.maximum(own_peak, jnp.max(suffix_scores, axis=-1)), own_start, 0
    )
    global_peak = lax.pmax(local_peak.reshape(rows_all, head_count), "seq")
    global_peak = global_peak.reshape(rows_all, heads_here, group_size)
    doc_accum, doc_totals = segment_terms(everyone, doc_member, global_peak, doc_keys, doc_values)
    leaf_accum, leaf_totals = segment_terms(
        everyone, leaf_member, global_peak, leaf_keys, leaf_values
    )
    accum = doc_accum + leaf_accum
    totals = doc_totals + leaf_totals
    own_top = lax.dynamic_slice_in_dim(global_peak, own_start, rows_here, 0)
    suffix_weights = jnp.exp(suffix_scores - own_top[..., None])
    suffix_accum = jnp.einsum(
        "rkgt,rtkh->rkgh",
        suffix_weights.astype(jnp.bfloat16),
        suffix_values,
        preferred_element_type=jnp.float32,
    )
    suffix_totals = jnp.sum(suffix_weights, axis=-1)
    accum = lax.dynamic_update_slice_in_dim(
        accum, lax.dynamic_slice_in_dim(accum, own_start, rows_here, 0) + suffix_accum, own_start, 0
    )
    totals = lax.dynamic_update_slice_in_dim(
        totals,
        lax.dynamic_slice_in_dim(totals, own_start, rows_here, 0) + suffix_totals,
        own_start,
        0,
    )
    accum_flat = accum.reshape(rows_all, head_count * HD)
    totals_flat = totals.reshape(rows_all, head_count)
    accum_own, totals_own = (
        lax.psum_scatter(accum_flat, "seq", scatter_dimension=0, tiled=True),
        lax.psum_scatter(totals_flat, "seq", scatter_dimension=0, tiled=True),
    )
    attention = lax.all_gather(
        normalized(accum_own, totals_own, head_count), "seq", axis=0, tiled=True
    )
    layer_out = lax.psum_scatter(
        jnp.dot(attention, out_weight, preferred_element_type=jnp.float32),
        "head",
        scatter_dimension=0,
        tiled=True,
    )
    return layer_out.astype(jnp.bfloat16)


def solution(mesh):
    in_specs = (
        P("seq", "head"),
        P(None, "seq", "head"),
        P(None, "seq", "head"),
        P(None, "seq", None, "head"),
        P("seq"),
        P(),
        P(),
        P("head", "seq"),
    )
    out_specs = P("head", "seq")
    return jax.shard_map(
        per_device, mesh=mesh, in_specs=in_specs, out_specs=out_specs, check_vma=False
    )
```

profile of v0, /device:TPU:1, one launch (start us, length us, event | category | flops | bytes accessed | tf_op | source)
XLA Modules:
  0.0 696.4 jit_solution(9763025174167249796)
XLA Ops:
  6.5 0.8 broadcast_compare_fusion
  7.3 0.8 select_reduce_fusion
  8.2 81.3 %all-gather = bf16[64,4,1024]{2,1,0:T(4,128)(2,1)S(1)} all-gather(bf16[1,4,1024]{2,1,0:T(4,128)(2,1)} %bitcast.263), channel_id=1, replica_groups=mesh['seq'=64,'head'=8] {'seq'}, dimensions={0}, use_global_device_ids=true | all-gather | bytes 532480 | tf_op jit(solution)/shard_map/all_gather | solution.py:86
  89.8 3.4 while.44
  89.9 0.8 fusion.77
  90.7 0.8 fusion.77
  91.6 0.8 fusion.77
  92.4 0.8 fusion.77
  93.3 0.5 copy-done.8
  93.9 0.7 slice_bitcast_fusion.2
  94.7 6.2 while.45
  94.7 1.6 fusion.80
  96.3 1.5 fusion.80
  97.8 1.5 fusion.80
  99.4 1.5 fusion.80
  101.7 114.7 %pmax.7 = f32[256,8]{0,1:T(8,128)S(1)} all-reduce(f32[256,8]{0,1:T(8,128)S(1)} %dynamic_update_slice.31), channel_id=1, replica_groups=mesh['seq'=64,'head'=8] {'seq'}, use_global_device_ids=true, to_apply=%region_8.9 | all-reduce | flops 2048 | bytes 16384 | tf_op jit(solution)/shard_map/pmax | solution.py:105
  216.7 10.6 %while.46 = (s32[]{:T(128)}, f32[4,64,1,8,128]{4,3,1,2,0:T(8,128)S(1)}, f32[4,64,1,8]{3,1,2,0:T(8,128)S(1)}, pred[4,64]{1,0:T(4,128)(4,1)}, bf16[4,64,1,8,128]{4...) while((s32[]{:T(128)}, ...), condition=%wide.region_11.12_spmd, body=%wide.region_9.11_spmd.sunk | while | flops 542113280 | bytes 5741305 | solution.py:58
  216.7 0.6 dynamic-slice_bitcast_fusion.15
  217.3 1.3 fusion.83
  218.6 0.7 fusion.84
  219.4 0.6 dynamic-slice_bitcast_fusion.15
  220.0 1.3 fusion.83
  221.3 0.7 fusion.84
  222.0 0.6 dynamic-slice_bitcast_fusion.15
  222.6 1.3 fusion.83
  223.9 0.7 fusion.84
  224.7 0.6 dynamic-slice_bitcast_fusion.15
  225.3 1.3 fusion.83
  226.6 0.7 fusion.84
  227.4 0.8 copy-done.5
  228.2 9.2 %while.47 = (s32[]{:T(128)}, f32[4,64,1,8,128]{4,3,1,2,0:T(8,128)S(1)}, f32[4,64,1,8]{3,1,2,0:T(8,128)S(1)}, pred[4,64]{1,0:T(4,128)(4,1)S(1)}, bf16[4,64,1,8,12...) while((s32[]{:T(128)}, ...), condition=%wide.region_14.15_spmd, body=%wide.region_12.14_spmd.sunk | while | flops 271056384 | bytes 3088697 | solution.py:58
  228.3 1.8 fusion.87
  230.6 1.8 fusion.87
  232.3 0.4 fusion.88
  232.9 1.8 fusion.87
  234.6 0.4 fusion.88
  235.1 1.8 fusion.87
  236.9 0.4 fusion.88
  237.6 1.1 copy-done.3
  238.9 1.2 copy.65
  240.8 1.3 dynamic-slice.4
  242.7 113.1 %all-reduce.1 = f32[256,8]{0,1:T(8,128)S(1)} all-reduce(f32[256,8]{0,1:T(8,128)S(1)} %dynamic_update_slice.33), channel_id=3, replica_groups=mesh['seq'=64,'head'=8] {'seq'}, use_global_device_ids=true, to_apply=%region_17.18.clone | all-reduce | flops 2048 | bytes 16384
  356.0 190.4 %all-reduce.4.cloned.1.call-done = f32[256,1024]{1,0:T(8,128)} async-done(((f32[256,1024]{1,0:T(8,128)}), f32[256,1024]{1,0:T(8,128)}) %all-reduce.4.cloned.1.call-update) | async-done | bytes 1048592
  546.4 0.8 fusion.52
  547.2 72.1 %all-gather.1 = bf16[64,4,1024]{2,1,0:T(4,128)(2,1)S(1)} all-gather(bf16[1,4,1024]{2,1,0:T(4,128)(2,1)S(1)} %fusion.52), channel_id=1, replica_groups=mesh['seq'=64,'head'=8] {'seq'}, dimensions={0}, use_global_device_ids=true | all-gather | bytes 532480 | tf_op jit(solution)/shard_map/all_gather | solution.py:137
  619.4 0.9 fusion.58
  620.3 67.9 %reduce-scatter.3.cloned.1.call-done = f32[32,128]{1,0:T(8,128)} async-done(((f32[256,128]{1,0:T(8,128)}), f32[32,128]{1,0:T(8,128)}) %reduce-scatter.3.cloned.1.call-update) | async-done | bytes 16400 | tf_op jit(solution)/shard_map/reduce_scatter | solution.py:140
  688.2 1.3 convert_element_type.18
  (89 shorter events, 3.8 us)
Async XLA Ops:
  6.5 612.8 %copy-start = (bf16[1024,128]{1,0:T(8,128)(2,1)S(1)}, bf16[1024,128]{1,0:T(8,128)(2,1)}, u32[]{:S(2)}) copy-start(bf16[1024,128]{1,0:T(8,128)(2,1)} %param.23) | copy-start | bytes 786436
  6.5 83.2 %copy-start.1 = (bf16[2,2048,128]{2,1,0:T(8,128)(2,1)S(1)}, bf16[2,2048,128]{2,1,0:T(8,128)(2,1)}, u32[]{:S(2)}) copy-start(bf16[2,2048,128]{2,1,0:T(8,128)(2,1)} %param.17) | copy-start | bytes 3145732
  6.5 539.9 %all-reduce.4.cloned.1.call-start = ((), (), s32[]{:S(2)}) async-start(), calls=%async_computation.2 | async-start | bytes 2097152
  89.8 4.0 copy-start.4
  93.3 0.5 copy-start.8
  94.6 6.3 copy-start.7
  94.6 6.4 copy-start.2
  94.6 6.4 copy-start.6
  227.3 0.8 copy-start.5
  237.5 1.2 copy-start.3
  240.2 448.1 %reduce-scatter.3.cloned.1.call-start = ((), (), s32[]{:S(2)}) async-start(), calls=%async_computation.1 | async-start | bytes 147456 | tf_op jit(solution)/shard_map/reduce_scatter | solution.py:140
Sparse Core Ops, SparseCore 0:
  240.3 306.0 all-reduce.3
  620.4 67.7 reduce-scatter.2
where the time goes:
time: 698 us; the launch traced here: 696 us
  blocking collectives  381 us (55%)
  waiting for transfers between devices  258 us (37%)
  matrix products  27.6 us (4%)
  between operations  14.3 us (2%)
  local copies, waits for them, and re-layouts  10.4 us (1%)
    unnamed x3, waiting for transfers between devices  190 us
    pmax x1, blocking collectives, per_device(): global_peak = lax.pmax(local_peak.reshape(rows_all, head_count), 'seq')  115 us
    unnamed x1, blocking collectives  113 us
    all_gather x1, blocking collectives, per_device(): everyone = split_heads(lax.all_gather(queries, 'seq', axis=0, tiled=True))  81.3 us
    all_gather x1, blocking collectives, per_device(): lax.all_gather(normalized(accum_own, totals_own, head_count), 'seq', axis...  72.1 us
    reduce_scatter x1, waiting for transfers between devices, per_device(): lax.psum_scatter(jnp.dot(attention, out_weight, preferred_element_type=jn...  67.9 us
    dot_general x16, matrix products, masked_scores(): jnp.einsum('bkgh,tkh->bkgt', query_block, key_rows, preferred_element_typ...  21.4 us
  transfers between devices with their start and end apart: 2, of which 2 were waited for; matrix products, arithmetic and copies ran while one was open for 0% of the time, Pallas kernels for 0%

commit v1 on v0

v1 whole, which is shorter than its diff:
```python
import jax
import jax.numpy as jnp
from jax import lax
from jax.experimental import pallas as pl
from jax.experimental.pallas import tpu as pltpu
from jax.sharding import PartitionSpec as P

MESH = pl.DeviceIdType.MESH
F32 = jnp.float32
BF16 = jnp.bfloat16
I32 = jnp.int32
NEG = -1e30
NX, NZ, NH = 4, 16, 8
HD = 128
G = 8
ROWS = 256
DOC_SLOTS = 48
LEAF_SLOTS = 12
SLOTS = 64
NT = (((1,), (1,)), ((), ()))
Z_ORDER = (8, 7, 9, 6, 10, 5, 11, 4, 12, 3, 13, 2, 14, 1, 15)


def iota(shape, dim):
    return lax.broadcasted_iota(I32, shape, dim)


def dot(a, b):
    return jnp.dot(a, b, preferred_element_type=F32)


def dot_nt(a, b):
    return lax.dot_general(a, b, NT, preferred_element_type=F32)


def onehot(cond):
    return jnp.where(cond, 1.0, 0.0).astype(BF16)


def softmax_parts(scores_of, chunks, chunk, lanes, vt_ref, s_ref, p_ref):
    top = None
    for c in range(chunks):
        s = scores_of(c)
        s_ref[c * chunk:(c + 1) * chunk, :lanes] = s
        peak = jnp.max(s, axis=0, keepdims=True)
        top = peak if top is None else jnp.maximum(top, peak)
    top = top.astype(BF16).astype(F32)
    total = None
    for c in range(chunks):
        p = jnp.exp(s_ref[c * chunk:(c + 1) * chunk, :lanes] - top)
        part = jnp.sum(p, axis=0, keepdims=True)
        total = part if total is None else total + part
        p_ref[c * chunk:(c + 1) * chunk, :lanes] = p.astype(BF16)
    accum = dot(vt_ref[...], p_ref[:chunks * chunk, :lanes])
    return top, total, accum


def kernel(q_ref, len_ref, parent_ref, rl_ref, doc_hbm, leaf_hbm, suf_hbm, w_hbm, out_ref,
           doc, leaf, suf, wv, doc_vt, leaf_vt, suf_vt, wt, qa, oh, ee, s_buf, p_buf, sb, rb, xs, xr, at, ob, db,
           ld, a_zs, a_zr, a_xs, a_xr, b_zs, b_zr, b_xs, b_xr, c_zs, c_zr, c_xs, c_xr, d_s, d_r):
    pos = lax.axis_index("seq")
    head = lax.axis_index("head")
    x, z = pos // NZ, pos % NZ
    quad = z // 4
    scaling = HD ** -0.5

    def at_xz(xx, zz):
        return (xx % NX) * NZ + zz % NZ

    def remote(src, dst, send, recv, seq_id, head_id):
        return pltpu.make_async_remote_copy(
            src_ref=src, dst_ref=dst, send_sem=send, recv_sem=recv,
            device_id=(seq_id, head_id), device_id_type=MESH)

    loads = [pltpu.make_async_copy(h, v, ld.at[i])
             for i, (h, v) in enumerate(((suf_hbm, suf), (doc_hbm, doc), (leaf_hbm, leaf), (w_hbm, wv)))]
    for load in loads:
        load.start()

    barrier = pltpu.get_barrier_semaphore()
    for o in Z_ORDER:
        pl.semaphore_signal(barrier, inc=1, device_id=(at_xz(x, z + o), head), device_id_type=MESH)
    for o in (1, 2, 3):
        pl.semaphore_signal(barrier, inc=1, device_id=(at_xz(x + o, z), head), device_id_type=MESH)
    for o in range(1, NH):
        pl.semaphore_signal(barrier, inc=1, device_id=(pos, (head + o) % NH), device_id_type=MESH)

    qf = q_ref[...].astype(F32)
    qa[pos] = jnp.concatenate([qf[:, g * HD:(g + 1) * HD] for g in range(G)], axis=0).astype(BF16)

    pl.semaphore_wait(barrier, 15 + 3 + 7)

    sends = []
    for o in Z_ORDER:
        c = remote(qa.at[pos], qa.at[pos], a_zs.at[o], a_zr.at[o], at_xz(x, z + o), head)
        c.start()
        sends.append(c)

    eye = onehot(iota((HD, HD), 0) == iota((HD, HD), 1))
    rl = rl_ref[...]
    leaf_hot = onehot(iota((64, ROWS), 0) == rl)
    parents = jnp.broadcast_to(parent_ref[...].astype(F32), (16, 64)).astype(BF16)
    rd = dot(parents, leaf_hot)[:1].astype(I32)
    before = onehot(iota((ROWS, ROWS), 0) < iota((ROWS, ROWS), 1))
    leaf_slot = jnp.sum(leaf_hot.astype(F32) * dot(leaf_hot, before), axis=0, keepdims=True).astype(I32)
    doc_hot = onehot(iota((16, ROWS), 0) == rd)
    doc_slot = jnp.sum(doc_hot.astype(F32) * dot(doc_hot, before), axis=0, keepdims=True).astype(I32)
    row = iota((1, ROWS), 1)

    my_doc = x * 4 + quad
    want = jnp.concatenate([
        jnp.where(rd == my_doc, doc_slot, 128),
        jnp.where(rl == pos, DOC_SLOTS + leaf_slot, 128),
        jnp.full((14, ROWS), 128, I32),
    ], axis=0).astype(F32).astype(BF16)
    for t in range(8):
        lane = iota((ROWS, 256), 1) + t * 256
        spread = onehot(iota((ROWS, 256), 0) == (lane // 32) * 4 + lane % 4)
        wide = dot(want, spread).astype(I32)
        lane = iota((1, 256), 1) + t * 256
        base = ((lane // 4) % 8) * SLOTS
        first = jnp.where(wide[0:1] < 128, wide[0:1] + base, -1)
        second = jnp.where(wide[1:2] < 128, wide[1:2] + base, -1)
        sub = iota((G * SLOTS, 256), 0)
        oh[:, t * 256:(t + 1) * 256] = onehot((sub == first) | (sub == second))

    sub = iota((ROWS, ROWS), 0)
    ee[0] = onehot(sub == jnp.where(rd // 4 == x, (rd % 4) * SLOTS + doc_slot, -1))
    for j in range(4):
        here = (rl // 16 == x) & (rl % 4 == j)
        ee[1 + j] = onehot(sub == jnp.where(here, ((rl // 4) % 4) * SLOTS + DOC_SLOTS + leaf_slot, -1))
        owner = row // 4
        here = (owner // 16 == x) & (owner % 4 == j)
        ee[5 + j] = onehot(sub == jnp.where(here, ((owner // 4) % 4) * SLOTS + 60 + row % 4, -1))

    loads[0].wait()
    for i in range(4):
        suf_vt[:, i * 512:(i + 1) * 512] = dot_nt(eye, suf[1, i]).astype(BF16)
    own_q = jnp.concatenate([qa[pos].astype(F32), jnp.zeros((96, HD), F32)], axis=0).astype(BF16)
    lane4 = iota((1, 128), 1) % 4
    live = jnp.where(lane4 == 0, len_ref[0], jnp.where(lane4 == 1, len_ref[1], jnp.where(
        lane4 == 2, len_ref[2], len_ref[3])))

    def suffix_scores(c):
        s = dot_nt(suf[0, c], own_q) * scaling
        return jnp.where((lane4 == c) & (iota((512, 128), 0) < live), s, NEG)

    top_s, total_s, accum_s = softmax_parts(suffix_scores, 4, 512, 128, suf_vt, s_buf, p_buf)

    def pieces(top, total):
        high = total.astype(BF16).astype(F32)
        return [top, high, total - high]

    packed = jnp.concatenate([accum_s] + pieces(top_s, total_s) + [jnp.zeros((13, 128), F32)], axis=0).astype(BF16)
    lane = iota((128, 512), 1)
    source = iota((128, 512), 0)
    place = onehot((lane % SLOTS >= 60) & (source == (lane // SLOTS) * 4 + lane % 4) & (source < 32))
    placed = dot(packed, place)

    loads[1].wait()
    for c in range(4):
        doc_vt[:, c * 512:(c + 1) * 512] = dot_nt(eye, doc[1, c * 512:(c + 1) * 512, :]).astype(BF16)
    loads[2].wait()
    for c in range(2):
        leaf_vt[:, c * 512:(c + 1) * 512] = dot_nt(eye, leaf[1, c * 512:(c + 1) * 512, :]).astype(BF16)
    loads[3].wait()
    for c in range(2):
        wt[:, c * 512:(c + 1) * 512] = dot_nt(eye, wv[c * 512:(c + 1) * 512, :]).astype(BF16)

    def z_wait(buf, index, send, recv, o):
        remote(buf.at[index], buf.at[index], send.at[o], recv.at[o], pos, head).wait_recv()

    for o in Z_ORDER[::-1]:
        z_wait(qa, at_xz(x, z - o), a_zs, a_zr, o)
    for k in range(4):
        part = qa.at[pl.ds(x * 16 + 4 * k, 4)]
        for o in (1, 2, 3):
            c = remote(part, part, a_xs.at[o * 4 + k], a_xr.at[o * 4 + k], at_xz(x + o, z), head)
            c.start()
            sends.append(c)
    for k in range(4):
        for o in (1, 2, 3):
            part = qa.at[pl.ds(((x - o) % NX) * 16 + 4 * k, 4)]
            remote(part, part, a_xs.at[o * 4 + k], a_xr.at[o * 4 + k], pos, head).wait_recv()

    every_q = qa[...].reshape(64 * 32, HD)
    slot_lane = iota((1, 256), 1) % SLOTS
    for hq in range(2):
        mine = dot(oh[hq * 256:(hq + 1) * 256, :], every_q).astype(BF16)
        top_d, total_d, accum_d = softmax_parts(
            lambda c: dot_nt(doc[0, c * 256:(c + 1) * 256, :], mine) * scaling, 8, 256, 256, doc_vt, s_buf, p_buf)
        top_l, total_l, accum_l = softmax_parts(
            lambda c: dot_nt(leaf[0, c * 256:(c + 1) * 256, :], mine) * scaling, 4, 256, 256, leaf_vt, s_buf, p_buf)
        stats = [
            jnp.where(slot_lane < DOC_SLOTS, d, jnp.where(slot_lane < 60, l, placed[HD + n:HD + n + 1, hq * 256:(hq + 1) * 256]))
            for n, (d, l) in enumerate(zip(pieces(top_d, total_d), pieces(top_l, total_l)))
        ]
        accum = jnp.where(slot_lane < DOC_SLOTS, accum_d, jnp.where(
            slot_lane < 60, accum_l, placed[:HD, hq * 256:(hq + 1) * 256])).astype(BF16)
        gap = jnp.zeros((5, 128), F32)
        stat = jnp.concatenate(
            [v[:, :128] for v in stats] + [gap] + [v[:, 128:] for v in stats] + [gap], axis=0).astype(BF16)
        for c in range(8):
            sb[hq * 8 + c, :, :256] = accum[c * 16:(c + 1) * 16]
            sb[hq * 8 + c, :, 256:] = stat

    for o in Z_ORDER:
        c = remote(sb.at[(z + o) % NZ], rb.at[z], b_zs.at[o], b_zr.at[o], at_xz(x, z + o), head)
        c.start()
        sends.append(c)
    rb[z] = sb[z]
    for o in Z_ORDER[::-1]:
        z_wait(rb, (z - o) % NZ, b_zs, b_zr, o)

    low = iota((16, 128), 1) < 64
    docs, rest = [], None
    for j in range(4):
        got = [rb[4 * k + j].astype(F32) for k in range(4)]
        left = []
        for b, t in ((0, 0), (1, 0), (0, 1), (1, 1), (0, 2), (1, 2)):
            tiles = [v[:, t * 128:(t + 1) * 128] for v in got]
            turned = [pltpu.roll(v, 64, 1) for v in tiles]
            if b == 0:
                halves = [jnp.where(low, tiles[0], turned[1]), jnp.where(low, tiles[2], turned[3])]
            else:
                halves = [jnp.where(low, turned[0], tiles[1]), jnp.where(low, turned[2], tiles[3])]
            left.append(jnp.concatenate(halves, axis=1))
        left = jnp.concatenate(left, axis=0).astype(BF16)
        docs.append(dot(left, ee[0]))
        more = (dot(left, ee[1 + j]), dot(left, ee[5 + j]))
        rest = more if rest is None else (rest[0] + more[0], rest[1] + more[1])

    def merged(parts):
        top = parts[0][1]
        for _, m, _ in parts[1:]:
            top = jnp.maximum(top, m)
        accum, total = None, None
        for a, m, l in parts:
            weight = jnp.exp(m - top)
            accum = a * weight if accum is None else accum + a * weight
            total = l * weight if total is None else total + l * weight
        return accum, top, total

    for a in range(4):
        t, b = a // 2, a % 2
        parts = []
        for got in docs + list(rest):
            s0 = 64 + b * 16 + t * 8
            total = got[s0 + 1:s0 + 2] + got[s0 + 2:s0 + 3]
            parts.append((got[a * 16:(a + 1) * 16], jnp.where(total > 0, got[s0:s0 + 1], NEG), total))
        accum, top, total = merged(parts)
        xs[a] = jnp.concatenate([accum, top, total, jnp.zeros((6, ROWS), F32)], axis=0)

    for o in (2, 1, 3):
        c = remote(xs.at[(x + o) % NX], xr.at[x], b_xs.at[o], b_xr.at[o], at_xz(x + o, z), head)
        c.start()
        sends.append(c)
    xr[x] = xs[x]
    for o in (1, 3, 2):
        z_wait(xr, (x - o) % NX, b_xs, b_xr, o)
    parts = []
    for i in range(NX):
        v = xr[i]
        parts.append((v[:16], v[16:17], v[17:18]))
    accum, _, total = merged(parts)

    def at_index(xx, zz):
        return (zz // 8) * 32 + xx * 8 + zz % 8

    mine = at_index(x, z)
    at[mine] = (accum / total).astype(BF16)
    for o in Z_ORDER:
        c = remote(at.at[mine], at.at[mine], c_zs.at[o], c_zr.at[o], at_xz(x, z + o), head)
        c.start()
        sends.append(c)
    for o in Z_ORDER[::-1]:
        z_wait(at, at_index(x, (z - o) % NZ), c_zs, c_zr, o)
    for k in range(2):
        part = at.at[pl.ds(k * 32 + x * 8, 8)]
        for o in (1, 2, 3):
            c = remote(part, part, c_xs.at[o * 2 + k], c_xr.at[o * 2 + k], at_xz(x + o, z), head)
            c.start()
            sends.append(c)
    for k in range(2):
        for o in (1, 2, 3):
            part = at.at[pl.ds(k * 32 + ((x - o) % NX) * 8, 8)]
            remote(part, part, c_xs.at[o * 2 + k], c_xr.at[o * 2 + k], pos, head).wait_recv()

    share = dot(wt[...], at[...].reshape(1024, ROWS)).T
    for i in range(NH):
        ob[i] = share[i * 32:(i + 1) * 32]
    for o in (4, 3, 5, 2, 6, 1, 7):
        c = remote(ob.at[(head + o) % NH], db.at[head], d_s.at[o], d_r.at[o], pos, (head + o) % NH)
        c.start()
        sends.append(c)
    db[head] = ob[head]
    for o in (1, 7, 2, 6, 3, 5, 4):
        z_wait(db, (head - o) % NH, d_s, d_r, o)
    out = db[0]
    for i in range(1, NH):
        out = out + db[i]
    out_ref[...] = out.astype(BF16)
    for c in sends:
        c.wait_send()


def per_device(queries, doc_kv, leaf_kv, suffix_kv, suffix_len, parent, row_leaf, out_weight):
    vmem = pl.BlockSpec(memory_space=pltpu.VMEM)
    smem = pl.BlockSpec(memory_space=pltpu.SMEM)
    hbm = pl.BlockSpec(memory_space=pl.ANY)
    dma = pltpu.SemaphoreType.DMA
    return pl.pallas_call(
        kernel,
        out_shape=jax.ShapeDtypeStruct((32, 128), BF16),
        in_specs=[vmem, smem, vmem, vmem, hbm, hbm, hbm, hbm],
        out_specs=vmem,
        scratch_shapes=[
            pltpu.VMEM((2, 2048, HD), BF16),
            pltpu.VMEM((2, 1024, HD), BF16),
            pltpu.VMEM((2, 4, 512, HD), BF16),
            pltpu.VMEM((1024, 128), BF16),
            pltpu.VMEM((HD, 2048), BF16),
            pltpu.VMEM((HD, 1024), BF16),
            pltpu.VMEM((HD, 2048), BF16),
            pltpu.VMEM((128, 1024), BF16),
            pltpu.VMEM((64, 32, HD), BF16),
            pltpu.VMEM((512, 2048), BF16),
            pltpu.VMEM((9, ROWS, ROWS), BF16),
            pltpu.VMEM((2048, 256), F32),
            pltpu.VMEM((2048, 256), BF16),
            pltpu.VMEM((16, 16, 384), BF16),
            pltpu.VMEM((16, 16, 384), BF16),
            pltpu.VMEM((4, 24, ROWS), F32),
            pltpu.VMEM((4, 24, ROWS), F32),
            pltpu.VMEM((64, 16, ROWS), BF16),
            pltpu.VMEM((8, 32, 128), F32),
            pltpu.VMEM((8, 32, 128), F32),
            dma((4,)),
            dma((16,)), dma((16,)), dma((16,)), dma((16,)),
            dma((16,)), dma((16,)), dma((4,)), dma((4,)),
            dma((16,)), dma((16,)), dma((8,)), dma((8,)),
            dma((8,)), dma((8,)),
        ],
        compiler_params=pltpu.CompilerParams(
            collective_id=0, has_side_effects=True, vmem_limit_bytes=48 << 20),
        name="tree_attention",
    )(queries, suffix_len, parent.reshape(1, -1), row_leaf.reshape(1, -1), doc_kv, leaf_kv, suffix_kv, out_weight)


def solution(mesh):
    in_specs = (
        P("seq", "head"),
        P(None, "seq", "head"),
        P(None, "seq", "head"),
        P(None, "seq", None, "head"),
        P("seq"),
        P(),
        P(),
        P("head", "seq"),
    )
    return jax.shard_map(
        per_device, mesh=mesh, in_specs=in_specs, out_specs=P("head", "seq"), check_vma=False)
```

time: 698 us -> 78.5 us (0.11)
  blocking collectives: 381 us -> 0 us
  waiting for transfers between devices: 258 us -> 0 us
  Pallas kernels: 0 us -> 71.8 us
  matrix products: 27.6 us -> 0 us
  between operations: 14.3 us -> 0.02 us
    unnamed x3 -> x0, waiting for transfers between devices: 190 us -> none
    all_gather x2 -> x0, blocking collectives: 153 us -> none  [the longest x1 81.3 us: per_device(): everyone = split_heads(lax.all_gather(queries, 'seq', axis=0, tiled=True))]
    pmax x1 -> x0, blocking collectives: 115 us -> none  [per_device(): global_peak = lax.pmax(local_peak.reshape(rows_all, head_count), 'seq')]
    unnamed x1 -> x0, blocking collectives: 113 us -> none
    pallas_call x0 -> x1, Pallas kernels: none -> 71.8 us  [per_device(): pl.pallas_call(kernel, out_shape=jax.ShapeDtypeStruct((32, 128), BF16), i...]
    reduce_scatter x1 -> x0, waiting for transfers between devices: 67.9 us -> none  [per_device(): lax.psum_scatter(jnp.dot(attention, out_weight, preferred_element_type=jn...]
    dot_general x27 -> x0, matrix products: 27.6 us -> none  [the longest x16 21.4 us: masked_scores(): jnp.einsum('bkgh,tkh->bkgt', query_block, key_rows, preferred_element_typ...]
  transfers between devices with their start and end apart: 2 -> 0, of which waited for: 2 -> 0; matrix products, arithmetic and copies ran while one was open for 0% -> 0% of each run, Pallas kernels for 0% -> 0%
where the time goes in v1:
time: 78.5 us; the launch traced here: 78.2 us
  Pallas kernels  71.8 us (91%)
  local copies, waits for them, and re-layouts  6.43 us (8%)
    pallas_call x1, Pallas kernels, per_device(): pl.pallas_call(kernel, out_shape=jax.ShapeDtypeStruct((32, 128), BF16), i...  71.8 us
    unnamed x17, local copies, waits for them, and re-layouts  6.43 us

profile of v1, /device:TPU:1, one launch (start us, length us, event | category | flops | bytes accessed | tf_op | source)
XLA Modules:
  0.0 78.2 jit_solution(13043763794057360511)
XLA Ops:
  0.0 0.0 copy-start.7
  0.0 0.0 copy-start.5
  0.0 0.0 copy-start.6
  0.0 0.6 copy-done.7
  0.7 0.0 copy-done.5
  0.7 0.0 copy-done.6
  0.7 0.0 copy-start
  0.7 1.2 %copy-done = bf16[2,2048,128]{2,1,0:T(8,128)(2,1)S(1)} copy-done((bf16[2,2048,128]{2,1,0:T(8,128)(2,1)S(1)}, bf16[2,2048,128]{2,1,0:T(8,128)(2,1)}, u32[]{:S(2)}) %copy-start) | copy-done | bytes 1048600
  1.9 0.0 copy-start.1
  1.9 1.2 %copy-done.1 = bf16[2,4,512,128]{3,2,1,0:T(8,128)(2,1)S(1)} copy-done((bf16[2,4,512,128]{3,2,1,0:T(8,128)(2,1)S(1)}, bf16[2,4,512,128]{3,2,1,0:T(8,128)(2,1)}, u32[]{:S(2)}) %copy-start.1) | copy-done | bytes 1048600
  3.1 0.0 copy-start.2
  3.2 1.0 %copy-done.2 = bf16[2,1024,128]{2,1,0:T(8,128)(2,1)S(1)} copy-done((bf16[2,1024,128]{2,1,0:T(8,128)(2,1)S(1)}, bf16[2,1024,128]{2,1,0:T(8,128)(2,1)}, u32[]{:S(2)}) %copy-start.2) | copy-done | bytes 524312
  4.2 0.0 copy-start.3
  4.2 0.9 %copy-done.3 = bf16[1024,128]{1,0:T(8,128)(2,1)S(1)} copy-done((bf16[1024,128]{1,0:T(8,128)(2,1)S(1)}, bf16[1024,128]{1,0:T(8,128)(2,1)}, u32[]{:S(2)}) %copy-start.3) | copy-done | bytes 262168
  5.1 0.0 copy-start.4
  5.1 0.7 copy-done.4
  5.8 71.8 %tree_attention.1 = bf16[32,128]{1,0:T(8,128)(2,1)S(1)} custom-call(bf16[4,1024]{1,0:T(4,128)(2,1)S(1)} %copy-done.4, s32[4]{0:T(128)S(1)} %copy-done.6, s32[1,64]{1,0:T(1,128)S(1)} %bitcast.3, s32[1,256]{1,0:T(1,128)S(1)} %bitcast.2, bf16[2,2048,128]{2,1,0:T(8,128)(2,1)S(1)} %copy-done, bf16[2,1024,128]{2,1,0:T(8,128)(2,1)S(1)} %copy-done.2, ...), custom_call_target="tpu_custom_call" | custom-call | tf_op jit(solution)/shard_map/tree_attention/pallas_call | solution.py:312
  77.6 0.6 copy.10
Async XLA Ops:
  0.0 0.7 copy-start.7
  0.0 0.7 copy-start.5
  0.0 0.7 copy-start.6
  0.7 1.2 %copy-start = (bf16[2,2048,128]{2,1,0:T(8,128)(2,1)S(1)}, bf16[2,2048,128]{2,1,0:T(8,128)(2,1)}, u32[]{:S(2)}) copy-start(bf16[2,2048,128]{2,1,0:T(8,128)(2,1)} %doc_hbm.1) | copy-start | bytes 3145732
  1.9 1.2 %copy-start.1 = (bf16[2,4,512,128]{3,2,1,0:T(8,128)(2,1)S(1)}, bf16[2,4,512,128]{3,2,1,0:T(8,128)(2,1)}, u32[]{:S(2)}) copy-start(bf16[2,4,512,128]{3,2,1,0:T(8,128)(2,1)} %suf_hbm.1) | copy-start | bytes 3145732
  3.1 1.0 %copy-start.2 = (bf16[2,1024,128]{2,1,0:T(8,128)(2,1)S(1)}, bf16[2,1024,128]{2,1,0:T(8,128)(2,1)}, u32[]{:S(2)}) copy-start(bf16[2,1024,128]{2,1,0:T(8,128)(2,1)} %leaf_hbm.1) | copy-start | bytes 1572868
  4.2 0.9 %copy-start.3 = (bf16[1024,128]{1,0:T(8,128)(2,1)S(1)}, bf16[1024,128]{1,0:T(8,128)(2,1)}, u32[]{:S(2)}) copy-start(bf16[1024,128]{1,0:T(8,128)(2,1)} %w_hbm.1) | copy-start | bytes 786436
  5.1 0.7 copy-start.4

commit v2 on v1

v2 whole, which is shorter than its diff:
```python
import jax
import jax.numpy as jnp
from jax import lax
from jax.experimental import pallas as pl
from jax.experimental.pallas import tpu as pltpu
from jax.sharding import PartitionSpec as P

MESH = pl.DeviceIdType.MESH
F32 = jnp.float32
BF16 = jnp.bfloat16
I32 = jnp.int32
NEG = -1e30
NX, NZ, NH = 4, 16, 8
HD = 128
G = 8
ROWS = 256
DOC_SLOTS = 48
LEAF_SLOTS = 12
RATE = HD ** -0.5 * 1.4426950408889634
SLOTS = 64
NT = (((1,), (1,)), ((), ()))
Z_FAR = (8, 7, 9, 6, 10, 5, 11, 4, 12, 3, 13, 2, 14, 1, 15)
Z_NEAR = Z_FAR[::-1]
Z_STEP = (4, 12, 3, 13, 2, 14, 1, 15)


def iota(shape, dim):
    return lax.broadcasted_iota(I32, shape, dim)


def dot(a, b):
    return jnp.dot(a, b, preferred_element_type=F32)


def dot_nt(a, b):
    return lax.dot_general(a, b, NT, preferred_element_type=F32)


def onehot(cond):
    return jnp.where(cond, 1.0, 0.0).astype(BF16)


def softmax_parts(scores_of, chunks, chunk, lanes, vt_ref, s_ref, p_ref):
    top = None
    for c in range(chunks):
        s = scores_of(c)
        s_ref[c * chunk:(c + 1) * chunk, :lanes] = s
        peak = jnp.max(s, axis=0, keepdims=True)
        top = peak if top is None else jnp.maximum(top, peak)
    top = top.astype(BF16).astype(F32)
    total = None
    for c in range(chunks):
        p = jnp.exp2(s_ref[c * chunk:(c + 1) * chunk, :lanes] * RATE - top * RATE)
        part = jnp.sum(p, axis=0, keepdims=True)
        total = part if total is None else total + part
        p_ref[c * chunk:(c + 1) * chunk, :lanes] = p.astype(BF16)
    accum = dot(vt_ref[...], p_ref[:chunks * chunk, :lanes])
    return top, total, accum


def kernel(q_hbm, len_ref, parent_hbm, rl_hbm, doc_hbm, leaf_hbm, suf_hbm, w_hbm, out_ref,
           q_ref, parent_ref, rl_ref, doc, leaf, suf, wv, doc_vt, leaf_vt, suf_vt, wx, qa, oh, ee, s_buf, p_buf, sb, rb, xs, xr, at, ob, db,
           ld, a_zs, a_zr, a_xs, a_xr, b_zs, b_zr, b_xs, b_xr, c_zs, c_zr, w_s, w_r, d_s, d_r):
    pos = lax.axis_index("seq")
    head = lax.axis_index("head")
    x, z = pos // NZ, pos % NZ
    quad = z // 4

    def at_xz(xx, zz):
        return (xx % NX) * NZ + zz % NZ

    def remote(src, dst, send, recv, seq_id, head_id):
        return pltpu.make_async_remote_copy(
            src_ref=src, dst_ref=dst, send_sem=send, recv_sem=recv,
            device_id=(seq_id, head_id), device_id_type=MESH)

    loads = [pltpu.make_async_copy(h, v, ld.at[i])
             for i, (h, v) in enumerate((
                 (suf_hbm, suf), (doc_hbm, doc), (leaf_hbm, leaf), (w_hbm, wv), (q_hbm, q_ref),
                 (parent_hbm, parent_ref), (rl_hbm, rl_ref)))]
    for i in (4, 5, 6, 0, 1, 2, 3):
        loads[i].start()

    barrier = pltpu.get_barrier_semaphore()
    for o in Z_STEP:
        pl.semaphore_signal(barrier, inc=1, device_id=(at_xz(x, z + o), head), device_id_type=MESH)
    for i in range(NX):
        for o in range(NH):
            if i or o:
                pl.semaphore_signal(
                    barrier, inc=1, device_id=(at_xz(x + i, z), (head + o) % NH), device_id_type=MESH)

    loads[4].wait()
    qf = q_ref[...].astype(F32)
    qa[pos] = jnp.concatenate([qf[:, g * HD:(g + 1) * HD] for g in range(G)], axis=0).astype(BF16)

    eye = onehot(iota((HD, HD), 0) == iota((HD, HD), 1))
    loads[5].wait()
    loads[6].wait()
    rl = rl_ref[...]
    leaf_hot = onehot(iota((64, ROWS), 0) == rl)
    parents = jnp.broadcast_to(parent_ref[...].astype(F32), (16, 64)).astype(BF16)
    rd = dot(parents, leaf_hot)[:1].astype(I32)
    before = onehot(iota((ROWS, ROWS), 0) < iota((ROWS, ROWS), 1))
    leaf_slot = jnp.sum(leaf_hot.astype(F32) * dot(leaf_hot, before), axis=0, keepdims=True).astype(I32)
    doc_hot = onehot(iota((16, ROWS), 0) == rd)
    doc_slot = jnp.sum(doc_hot.astype(F32) * dot(doc_hot, before), axis=0, keepdims=True).astype(I32)
    row = iota((1, ROWS), 1)

    my_doc = x * 4 + quad
    want = jnp.concatenate([
        jnp.where(rd == my_doc, doc_slot, 128),
        jnp.where(rl == pos, DOC_SLOTS + leaf_slot, 128),
        jnp.full((14, ROWS), 128, I32),
    ], axis=0).astype(F32).astype(BF16)
    for t in range(8):
        lane = iota((ROWS, 256), 1) + t * 256
        spread = onehot(iota((ROWS, 256), 0) == (lane // 32) * 4 + lane % 4)
        wide = dot(want, spread).astype(I32)
        lane = iota((1, 256), 1) + t * 256
        base = ((lane // 4) % 8) * SLOTS
        first = jnp.where(wide[0:1] < 128, wide[0:1] + base, -1)
        second = jnp.where(wide[1:2] < 128, wide[1:2] + base, -1)
        sub = iota((G * SLOTS, 256), 0)
        oh[:, t * 256:(t + 1) * 256] = onehot((sub == first) | (sub == second))

    pl.semaphore_wait(barrier, len(Z_STEP) + NX * NH - 1)

    sends = []

    def push(src, dst, send, recv, seq_id, head_id):
        c = remote(src, dst, send, recv, seq_id, head_id)
        c.start()
        sends.append(c)

    for o in Z_STEP:
        push(qa.at[pos], qa.at[pos], a_zs.at[16 - o], a_zr.at[16 - o], at_xz(x, z + o), head)
    for r in (0, 1, 15, 2, 14, 3, 13, 4, 12, 5, 11, 6, 10, 7, 9, 8):
        block = qa.at[at_xz(x, z + r)]
        if r:
            remote(block, block, a_zs.at[r], a_zr.at[r], pos, head).wait_recv()
        if 1 <= r <= 4:
            push(block, block, a_zs.at[r + 4], a_zr.at[r + 4], at_xz(x, z - 4), head)
        if 13 <= r <= 15:
            push(block, block, a_zs.at[r - 4], a_zr.at[r - 4], at_xz(x, z + 4), head)
        for i in (2, 1, 3):
            push(block, block, a_xs.at[i * 16 + r], a_xr.at[i * 16 + r], at_xz(x + i, z), head)

    loads[0].wait()
    for i in range(4):
        suf_vt[:, i * 512:(i + 1) * 512] = dot_nt(eye, suf[1, i]).astype(BF16)
    own_q = jnp.concatenate([qa[pos].astype(F32), jnp.zeros((96, HD), F32)], axis=0).astype(BF16)
    lane4 = iota((1, 128), 1) % 4
    live = jnp.where(lane4 == 0, len_ref[0], jnp.where(lane4 == 1, len_ref[1], jnp.where(
        lane4 == 2, len_ref[2], len_ref[3])))

    def suffix_scores(c):
        s = dot_nt(suf[0, c], own_q)
        return jnp.where((lane4 == c) & (iota((512, 128), 0) < live), s, NEG)

    top_s, total_s, accum_s = softmax_parts(suffix_scores, 4, 512, 128, suf_vt, s_buf, p_buf)

    def pieces(top, total):
        high = total.astype(BF16).astype(F32)
        return [top, high, total - high]

    packed = jnp.concatenate([accum_s] + pieces(top_s, total_s) + [jnp.zeros((13, 128), F32)], axis=0).astype(BF16)
    lane = iota((128, 512), 1)
    source = iota((128, 512), 0)
    place = onehot((lane % SLOTS >= 60) & (source == (lane // SLOTS) * 4 + lane % 4) & (source < 32))
    placed = dot(packed, place)

    loads[1].wait()
    for c in range(4):
        doc_vt[:, c * 512:(c + 1) * 512] = dot_nt(eye, doc[1, c * 512:(c + 1) * 512, :]).astype(BF16)
    loads[2].wait()
    for c in range(2):
        leaf_vt[:, c * 512:(c + 1) * 512] = dot_nt(eye, leaf[1, c * 512:(c + 1) * 512, :]).astype(BF16)
    for r in range(16):
        for i in (1, 3, 2):
            block = qa.at[at_xz(x - i, z + r)]
            remote(block, block, a_xs.at[i * 16 + r], a_xr.at[i * 16 + r], pos, head).wait_recv()

    every_q = qa[...].reshape(64 * 32, HD)
    slot_lane = iota((1, 256), 1) % SLOTS
    for hq in range(2):
        mine = dot(oh[hq * 256:(hq + 1) * 256, :], every_q).astype(BF16)
        top_d, total_d, accum_d = softmax_parts(
            lambda c: dot_nt(doc[0, c * 256:(c + 1) * 256, :], mine), 8, 256, 256, doc_vt, s_buf, p_buf)
        top_l, total_l, accum_l = softmax_parts(
            lambda c: dot_nt(leaf[0, c * 256:(c + 1) * 256, :], mine), 4, 256, 256, leaf_vt, s_buf, p_buf)
        stats = [
            jnp.where(slot_lane < DOC_SLOTS, d, jnp.where(slot_lane < 60, l, placed[HD + n:HD + n + 1, hq * 256:(hq + 1) * 256]))
            for n, (d, l) in enumerate(zip(pieces(top_d, total_d), pieces(top_l, total_l)))
        ]
        accum = jnp.where(slot_lane < DOC_SLOTS, accum_d, jnp.where(
            slot_lane < 60, accum_l, placed[:HD, hq * 256:(hq + 1) * 256])).astype(BF16)
        gap = jnp.zeros((5, 128), F32)
        stat = jnp.concatenate(
            [v[:, :128] for v in stats] + [gap] + [v[:, 128:] for v in stats] + [gap], axis=0).astype(BF16)
        for c in range(8):
            sb[hq * 8 + c, :, :256] = accum[c * 16:(c + 1) * 16]
            sb[hq * 8 + c, :, 256:] = stat
        for c in range(8):
            to = hq * 8 + (z + 4 + c) % 8

            @pl.when(to != z)
            def _():
                remote(sb.at[to], rb.at[z], b_zs.at[to], b_zr.at[z], at_xz(x, to), head).start()

    loads[3].wait()
    for o in (2, 1, 3):
        push(wv.at[:, (x + o) % NX], wx.at[x], w_s.at[o], w_r.at[o], at_xz(x + o, z), head)
    wx[x] = wv[:, x]

    sub = iota((ROWS, ROWS), 0)
    ee[0] = onehot(sub == jnp.where(rd // 4 == x, (rd % 4) * SLOTS + doc_slot, -1))
    for j in range(4):
        here = (rl // 16 == x) & (rl % 4 == j)
        ee[1 + j] = onehot(sub == jnp.where(here, ((rl // 4) % 4) * SLOTS + DOC_SLOTS + leaf_slot, -1))
        owner = row // 4
        here = (owner // 16 == x) & (owner % 4 == j)
        ee[5 + j] = onehot(sub == jnp.where(here, ((owner // 4) % 4) * SLOTS + 60 + row % 4, -1))

    rb[z] = sb[z]
    for o in Z_NEAR:
        i = (z - o) % NZ
        c = remote(sb.at[i], rb.at[i], b_zs.at[i], b_zr.at[i], pos, head)
        c.wait_send()
        c.wait_recv()

    low = iota((16, 128), 1) < 64
    docs, rest = [], None
    for j in range(4):
        got = [rb[4 * k + j].astype(F32) for k in range(4)]
        left = []
        for b, t in ((0, 0), (1, 0), (0, 1), (1, 1), (0, 2), (1, 2)):
            tiles = [v[:, t * 128:(t + 1) * 128] for v in got]
            turned = [pltpu.roll(v, 64, 1) for v in tiles]
            if b == 0:
                halves = [jnp.where(low, tiles[0], turned[1]), jnp.where(low, tiles[2], turned[3])]
            else:
                halves = [jnp.where(low, turned[0], tiles[1]), jnp.where(low, turned[2], tiles[3])]
            left.append(jnp.concatenate(halves, axis=1))
        left = jnp.concatenate(left, axis=0).astype(BF16)
        docs.append(dot(left, ee[0]))
        more = (dot(left, ee[1 + j]), dot(left, ee[5 + j]))
        rest = more if rest is None else (rest[0] + more[0], rest[1] + more[1])

    def merged(parts):
        top = parts[0][1]
        for _, m, _ in parts[1:]:
            top = jnp.maximum(top, m)
        accum, total = None, None
        for a, m, l in parts:
            weight = jnp.exp2((m - top) * RATE)
            accum = a * weight if accum is None else accum + a * weight
            total = l * weight if total is None else total + l * weight
        return accum, top, total

    for a in range(4):
        t, b = a // 2, a % 2
        parts = []
        for got in docs + list(rest):
            s0 = 64 + b * 16 + t * 8
            total = got[s0 + 1:s0 + 2] + got[s0 + 2:s0 + 3]
            parts.append((got[a * 16:(a + 1) * 16], jnp.where(total > 0, got[s0:s0 + 1], NEG), total))
        accum, top, total = merged(parts)
        xs[a] = jnp.concatenate([accum, top, total, jnp.zeros((6, ROWS), F32)], axis=0)

    for o in (2, 1, 3):
        push(xs.at[(x + o) % NX], xr.at[x], b_xs.at[o], b_xr.at[o], at_xz(x + o, z), head)
    xr[x] = xs[x]
    for o in (1, 3, 2):
        block = xr.at[(x - o) % NX]
        remote(block, block, b_xs.at[o], b_xr.at[o], pos, head).wait_recv()
    parts = []
    for i in range(NX):
        v = xr[i]
        parts.append((v[:16], v[16:17], v[17:18]))
    accum, _, total = merged(parts)

    at[z] = (accum / total).astype(BF16)
    for o in Z_FAR:
        push(at.at[z], at.at[z], c_zs.at[16 - o], c_zr.at[16 - o], at_xz(x, z + o), head)
    for o in (1, 3, 2):
        block = wx.at[(x - o) % NX]
        remote(block, block, w_s.at[o], w_r.at[o], pos, head).wait_recv()
    for r in Z_NEAR:
        block = at.at[(z + r) % NZ]
        remote(block, block, c_zs.at[r], c_zr.at[r], pos, head).wait_recv()

    eye = onehot(iota((ROWS, ROWS), 0) == iota((ROWS, ROWS), 1))
    attention = dot_nt(eye, at[...].reshape(ROWS, ROWS)).astype(BF16)
    for i in (2, 1, 3, 0):
        to = (x + i) % NX
        share = dot(attention, wx[to].reshape(2 * HD, HD)).astype(BF16)
        for n in range(NH):
            ob[to, n] = share[n * 32:(n + 1) * 32]
        for o in (4, 3, 5, 2, 6, 1, 7, 0):
            if i or o:
                n = (head + o) % NH
                push(ob.at[to, n], db.at[x, head], d_s.at[i * 8 + o], d_r.at[i * 8 + o], at_xz(to, z), n)
    db[x, head] = ob[x, head]
    for i in (1, 3, 2, 0):
        for o in range(NH):
            if i or o:
                block = db.at[(x - i) % NX, (head - o) % NH]
                remote(block, block, d_s.at[i * 8 + o], d_r.at[i * 8 + o], pos, head).wait_recv()
    out_ref[...] = jnp.sum(db[...].reshape(NX * NH, 32, HD).astype(F32), axis=0).astype(BF16)
    for c in sends:
        c.wait_send()


def per_device(queries, doc_kv, leaf_kv, suffix_kv, suffix_len, parent, row_leaf, out_weight):
    vmem = pl.BlockSpec(memory_space=pltpu.VMEM)
    smem = pl.BlockSpec(memory_space=pltpu.SMEM)
    hbm = pl.BlockSpec(memory_space=pl.ANY)
    dma = pltpu.SemaphoreType.DMA
    return pl.pallas_call(
        kernel,
        out_shape=jax.ShapeDtypeStruct((32, 128), BF16),
        in_specs=[hbm, smem, hbm, hbm, hbm, hbm, hbm, hbm],
        out_specs=vmem,
        scratch_shapes=[
            pltpu.VMEM((4, 1024), BF16),
            pltpu.VMEM((1, 64), I32),
            pltpu.VMEM((1, 256), I32),
            pltpu.VMEM((2, 2048, HD), BF16),
            pltpu.VMEM((2, 1024, HD), BF16),
            pltpu.VMEM((2, 4, 512, HD), BF16),
            pltpu.VMEM((2, NX, HD, HD), BF16),
            pltpu.VMEM((HD, 2048), BF16),
            pltpu.VMEM((HD, 1024), BF16),
            pltpu.VMEM((HD, 2048), BF16),
            pltpu.VMEM((NX, 2, HD, HD), BF16),
            pltpu.VMEM((64, 32, HD), BF16),
            pltpu.VMEM((512, 2048), BF16),
            pltpu.VMEM((9, ROWS, ROWS), BF16),
            pltpu.VMEM((2048, 256), F32),
            pltpu.VMEM((2048, 256), BF16),
            pltpu.VMEM((16, 16, 384), BF16),
            pltpu.VMEM((16, 16, 384), BF16),
            pltpu.VMEM((4, 24, ROWS), F32),
            pltpu.VMEM((4, 24, ROWS), F32),
            pltpu.VMEM((16, 16, ROWS), BF16),
            pltpu.VMEM((NX, NH, 32, HD), BF16),
            pltpu.VMEM((NX, NH, 32, HD), BF16),
            dma((7,)),
            dma((16,)), dma((16,)), dma((64,)), dma((64,)),
            dma((16,)), dma((16,)), dma((4,)), dma((4,)),
            dma((16,)), dma((16,)), dma((4,)), dma((4,)),
            dma((32,)), dma((32,)),
        ],
        compiler_params=pltpu.CompilerParams(
            collective_id=0, has_side_effects=True, vmem_limit_bytes=62 << 20),
        name="tree_attention",
    )(queries, suffix_len, parent.reshape(1, -1), row_leaf.reshape(1, -1), doc_kv, leaf_kv, suffix_kv,
      out_weight.reshape(2, NX, HD, HD))


def solution(mesh):
    in_specs = (
        P("seq", "head"),
        P(None, "seq", "head"),
        P(None, "seq", "head"),
        P(None, "seq", None, "head"),
        P("seq"),
        P(),
        P(),
        P("head", "seq"),
    )
    return jax.shard_map(
        per_device, mesh=mesh, in_specs=in_specs, out_specs=P("head", "seq"), check_vma=False)
```

time: 78.5 us -> 66.4 us (0.85)
  Pallas kernels: 71.8 us -> 64.9 us
  local copies, waits for them, and re-layouts: 6.43 us -> 1.3 us
    pallas_call x1, Pallas kernels: 71.8 us -> 64.9 us  [per_device(): pl.pallas_call(kernel, out_shape=jax.ShapeDtypeStruct((32, 128), BF16), i...]
    unnamed x17 -> x1, local copies, waits for them, and re-layouts: 6.43 us -> 1.3 us
where the time goes in v2:
time: 66.4 us; the launch traced here: 66.2 us
  Pallas kernels  64.9 us (98%)
  local copies, waits for them, and re-layouts  1.3 us (2%)
    pallas_call x1, Pallas kernels, per_device(): pl.pallas_call(kernel, out_shape=jax.ShapeDtypeStruct((32, 128), BF16), i...  64.9 us

profile of v2, /device:TPU:1, one launch (start us, length us, event | category | flops | bytes accessed | tf_op | source)
XLA Modules:
  0.0 66.2 jit_solution(7556628235064837286)
XLA Ops:
  0.0 64.9 %tree_attention.1 = bf16[32,128]{1,0:T(8,128)(2,1)} custom-call(bf16[4,1024]{1,0:T(4,128)(2,1)} %q_hbm.1, s32[4]{0:T(128)} %len_ref.1, s32[1,64]{1,0:T(1,128)} %bitcast.5, s32[1,256]{1,0:T(1,128)} %bitcast.4, bf16[2,2048,128]{2,1,0:T(8,128)(2,1)} %doc_hbm.1, bf16[2,1024,128]{2,1,0:T(8,128)(2,1)} %leaf_hbm.1, bf16[2,4,512,128]{3,2,1,0:T(8,128)(2,1)} %suf_hbm.1, ...), custom_call_target="tpu_custom_call" | custom-call | tf_op jit(solution)/shard_map/tree_attention/pallas_call | solution.py:320
  64.9 1.3 %copy.10 = bf16[32,128]{1,0:T(8,128)(2,1)} copy(bf16[32,128]{1,0:T(8,128)(2,1)} %tree_attention.1) | data formatting | bytes 16384

commit v3 on v2

v3 whole, which is shorter than its diff:
```python
import jax
import jax.numpy as jnp
from jax import lax
from jax.experimental import pallas as pl
from jax.experimental.pallas import tpu as pltpu
from jax.sharding import PartitionSpec as P

MESH = pl.DeviceIdType.MESH
F32 = jnp.float32
BF16 = jnp.bfloat16
I32 = jnp.int32
NEG = -2.0 ** 100
NX, NZ, NH = 4, 16, 8
HD = 128
G = 8
ROWS = 256
DOC_SLOTS = 48
LEAF_SLOTS = 12
RATE = HD ** -0.5 * 1.4426950408889634
LEAF_AT = G // 2 * DOC_SLOTS
NT = (((1,), (1,)), ((), ()))
Z_FAR = (8, 7, 9, 6, 10, 5, 11, 4, 12, 3, 13, 2, 14, 1, 15)
Z_NEAR = Z_FAR[::-1]
Z_STEP = (4, 12, 3, 13, 2, 14, 1, 15)


def iota(shape, dim):
    return lax.broadcasted_iota(I32, shape, dim)


def dot(a, b):
    return jnp.dot(a, b, preferred_element_type=F32)


def dot_nt(a, b):
    return lax.dot_general(a, b, NT, preferred_element_type=F32)


def onehot(cond):
    return jnp.where(cond, 1.0, 0.0).astype(BF16)


def merged(parts):
    top = parts[0][1]
    for _, m, _ in parts[1:]:
        top = jnp.maximum(top, m)
    accum, total = None, None
    for a, m, l in parts:
        weight = jnp.exp2((m - top) * RATE)
        accum = a * weight if accum is None else accum + a * weight
        total = l * weight if total is None else total + l * weight
    return accum, top, total


def attend(scores_of, chunks, chunk, vt_ref):
    parts = []
    for c in range(chunks):
        s = scores_of(c)
        top = jnp.max(s, axis=0, keepdims=True)
        p = jnp.exp2(s * RATE - top * RATE)
        accum = dot(vt_ref[:, c * chunk:(c + 1) * chunk], p.astype(BF16))
        parts.append((accum, top, jnp.sum(p, axis=0, keepdims=True)))
    accum, top, total = merged(parts)
    level = top + jnp.log2(total) * (1 / RATE)
    high = level.astype(BF16).astype(F32)
    return accum / total, high, level - high


def turn(v, lanes):
    return pltpu.roll(v, lanes % 128, 1) if lanes % 128 else v


def kernel(q_hbm, len_ref, parent_hbm, rl_hbm, doc_hbm, leaf_hbm, suf_hbm, w_hbm, out_ref,
           q_ref, parent_ref, rl_ref, doc, leaf, suf, wv, doc_vt, leaf_vt, suf_vt, wx, qa, oh, ed, el, es, sl, rl_in, sb, rb, xs, xr, at, ob, db,
           ld, a_zs, a_zr, a_xs, a_xr, l_zs, l_zr, b_zs, b_zr, b_xs, b_xr, c_zs, c_zr, w_s, w_r, d_s, d_r):
    pos = lax.axis_index("seq")
    head = lax.axis_index("head")
    x, z = pos // NZ, pos % NZ
    quad = z // 4

    def at_xz(xx, zz):
        return (xx % NX) * NZ + zz % NZ

    def remote(src, dst, send, recv, seq_id, head_id):
        return pltpu.make_async_remote_copy(
            src_ref=src, dst_ref=dst, send_sem=send, recv_sem=recv,
            device_id=(seq_id, head_id), device_id_type=MESH)

    loads = [pltpu.make_async_copy(h, v, ld.at[i])
             for i, (h, v) in enumerate((
                 (suf_hbm, suf), (doc_hbm, doc), (leaf_hbm, leaf), (w_hbm, wv), (q_hbm, q_ref),
                 (parent_hbm, parent_ref), (rl_hbm, rl_ref)))]
    for i in (4, 5, 6, 0, 1, 2, 3):
        loads[i].start()

    barrier = pltpu.get_barrier_semaphore()
    for o in Z_STEP:
        pl.semaphore_signal(barrier, inc=1, device_id=(at_xz(x, z + o), head), device_id_type=MESH)
    for i in range(NX):
        for o in range(NH):
            if i or o:
                pl.semaphore_signal(
                    barrier, inc=1, device_id=(at_xz(x + i, z), (head + o) % NH), device_id_type=MESH)

    loads[4].wait()
    qf = q_ref[...].astype(F32)
    qa[pos] = jnp.concatenate([qf[:, g * HD:(g + 1) * HD] for g in range(G)], axis=0).astype(BF16)

    eye = onehot(iota((HD, HD), 0) == iota((HD, HD), 1))
    loads[5].wait()
    loads[6].wait()
    rl = rl_ref[...]
    leaf_hot = onehot(iota((64, ROWS), 0) == rl)
    parents = jnp.broadcast_to(parent_ref[...].astype(F32), (16, 64)).astype(BF16)
    rd = dot(parents, leaf_hot)[:1].astype(I32)
    before = onehot(iota((ROWS, ROWS), 0) < iota((ROWS, ROWS), 1))
    leaf_slot = jnp.sum(leaf_hot.astype(F32) * dot(leaf_hot, before), axis=0, keepdims=True).astype(I32)
    doc_hot = onehot(iota((16, ROWS), 0) == rd)
    doc_slot = jnp.sum(doc_hot.astype(F32) * dot(doc_hot, before), axis=0, keepdims=True).astype(I32)
    row = iota((1, ROWS), 1)

    my_doc = x * 4 + quad
    want = jnp.concatenate([
        jnp.where(rd == my_doc, doc_slot, 128),
        jnp.where(rl == pos, leaf_slot, 128),
        jnp.full((14, ROWS), 128, I32),
    ], axis=0).astype(F32).astype(BF16)
    for t in range(NX):
        lane = iota((ROWS, 256), 1)
        spread = onehot(iota((ROWS, 256), 0) == t * 64 + (lane // 16) * 4 + lane % 4)
        wide = dot(want, spread).astype(I32)
        a = (iota((1, 256), 1) // 4) % 4
        first = jnp.where(wide[0:1] < 128, wide[0:1] + a * DOC_SLOTS, -1)
        second = jnp.where(wide[1:2] < 128, wide[1:2] + (LEAF_AT + a * LEAF_SLOTS), -1)
        sub = iota((256, 256), 0)
        oh[t] = onehot((sub == first) | (sub == second))

    pl.semaphore_wait(barrier, len(Z_STEP) + NX * NH - 1)

    sends = []

    def push(src, dst, send, recv, seq_id, head_id):
        c = remote(src, dst, send, recv, seq_id, head_id)
        c.start()
        sends.append(c)

    for o in Z_STEP:
        push(qa.at[pos], qa.at[pos], a_zs.at[16 - o], a_zr.at[16 - o], at_xz(x, z + o), head)
    for r in (0, 1, 15, 2, 14, 3, 13, 4, 12, 5, 11, 6, 10, 7, 9, 8):
        block = qa.at[at_xz(x, z + r)]
        if r:
            remote(block, block, a_zs.at[r], a_zr.at[r], pos, head).wait_recv()
        if 1 <= r <= 4:
            push(block, block, a_zs.at[r + 4], a_zr.at[r + 4], at_xz(x, z - 4), head)
        if 13 <= r <= 15:
            push(block, block, a_zs.at[r - 4], a_zr.at[r - 4], at_xz(x, z + 4), head)
        for i in (2, 1, 3):
            push(block, block, a_xs.at[i * 16 + r], a_xr.at[i * 16 + r], at_xz(x + i, z), head)

    loads[0].wait()
    for i in range(4):
        suf_vt[:, i * 512:(i + 1) * 512] = dot_nt(eye, suf[1, i]).astype(BF16)
    own_q = jnp.concatenate([qa[pos].astype(F32), jnp.zeros((96, HD), F32)], axis=0).astype(BF16)
    lane4 = iota((1, 128), 1) % 4
    live = jnp.where(lane4 == 0, len_ref[0], jnp.where(lane4 == 1, len_ref[1], jnp.where(
        lane4 == 2, len_ref[2], len_ref[3])))

    def suffix_scores(c):
        s = dot_nt(suf[0, c], own_q)
        return jnp.where((lane4 == c) & (iota((512, 128), 0) < live), s, NEG)

    accum, high, low = attend(suffix_scores, 4, 512, suf_vt)

    def send_parts(out, into, send, recv, pair):
        def start(c):
            to = pair * 4 + (z + c) % 4
            remote(out.at[to], into.at[z], send.at[to], recv.at[z], at_xz(x, to), head).start()

        @pl.when(z // 4 == pair)
        def _():
            for c in (1, 2, 3):
                start(c)

        @pl.when(z // 4 != pair)
        def _():
            for c in range(4):
                start(c)

    lane = iota((1, 128), 1)
    stat = jnp.concatenate([high, low, jnp.zeros((14, 128), F32)], axis=0)
    for pair in range(4):
        a0, a1, v = turn(accum, -8 * pair), turn(accum, 8 - 8 * pair), turn(stat, 16 - 8 * pair)
        for c in range(4):
            sl[pair * 4 + c] = jnp.where(lane < 8, a0[c * 32:c * 32 + 16], jnp.where(
                lane < 16, a1[c * 32 + 16:c * 32 + 32], v)).astype(BF16)
        send_parts(sl, rl_in, l_zs, l_zr, pair)

    loads[1].wait()
    for c in range(4):
        doc_vt[:, c * 512:(c + 1) * 512] = dot_nt(eye, doc[1, c * 512:(c + 1) * 512, :]).astype(BF16)
    loads[2].wait()
    for c in range(2):
        leaf_vt[:, c * 512:(c + 1) * 512] = dot_nt(eye, leaf[1, c * 512:(c + 1) * 512, :]).astype(BF16)
    halves = [None, None]
    for i in (0, 1, 3, 2):
        plane = (x - i) % NX
        if i:
            for r in range(16):
                block = qa.at[at_xz(plane, z + r)]
                remote(block, block, a_xs.at[i * 16 + r], a_xr.at[i * 16 + r], pos, head).wait_recv()
        got = qa[pl.ds(plane * NZ, NZ)]
        for hq in range(2):
            more = dot(oh[plane], got[:, hq * 16:(hq + 1) * 16].reshape(256, HD))
            halves[hq] = more if halves[hq] is None else halves[hq] + more
    halves = [v.astype(BF16) for v in halves]
    rest = jnp.zeros((32, HD), BF16)

    mine = jnp.concatenate([halves[0][LEAF_AT:LEAF_AT + 48], halves[1][LEAF_AT:LEAF_AT + 48], rest], axis=0)
    accum, high, low = attend(lambda c: dot_nt(leaf[0, c * 512:(c + 1) * 512, :], mine), 2, 512, leaf_vt)
    packed = jnp.concatenate([accum, high, low, jnp.zeros((14, 128), F32)], axis=0).astype(BF16)
    source = iota((128, 512), 0)
    place = iota((128, 512), 1)
    leaf_part = dot(packed, onehot(
        (place % 128 >= 96) & (place % 128 < 120) & (source == (place // 128) * 24 + place % 128 - 96)))

    spread = iota((16, 128), 0) == iota((16, 128), 1) // 8
    spread = spread & (iota((16, 128), 1) < 120)
    gather = onehot((iota((128, 128), 1) >= 120) & (iota((128, 128), 0) % 8 == iota((128, 128), 1) - 120))
    for pair in range(4):
        mine = jnp.concatenate([halves[pair // 2][(pair % 2) * 96:(pair % 2) * 96 + 96], rest], axis=0)
        accum, high, low = attend(lambda c: dot_nt(doc[0, c * 512:(c + 1) * 512, :], mine), 4, 512, doc_vt)
        other = leaf_part[:, pair * 128:(pair + 1) * 128]
        accum = jnp.where(lane < 96, accum, other[:HD])
        high = jnp.where(lane < 96, high, other[HD:HD + 1])
        low = jnp.where(lane < 96, low, other[HD + 1:HD + 2])
        both = jnp.concatenate([jnp.where(spread, high, 0.0), jnp.where(spread, low, 0.0)], axis=0).astype(BF16)
        both = dot(both, gather)
        for c in range(4):
            sb[pair * 4 + c] = jnp.where(lane < 120, accum[c * 32:(c + 1) * 32], both).astype(BF16)
        send_parts(sb, rb, b_zs, b_zr, pair)

    loads[3].wait()
    for o in (2, 1, 3):
        to = (x + o) % NX
        push(wv.at[:, to // 2, :, to % 2], wx.at[x], w_s.at[o], w_r.at[o], at_xz(x + o, z), head)
    wx[x] = wv[:, x // 2, :, x % 2]

    sub = iota((512, ROWS), 0)
    for b in range(2):
        cols = slice(b * ROWS, (b + 1) * ROWS)
        ed[:, cols] = onehot(sub == jnp.where(rd // 4 == x, (rd % 4) * 128 + b * DOC_SLOTS + doc_slot, -1))
        el[:, cols] = onehot(sub == jnp.where(
            rl // 16 == x, (rl % 4) * 128 + (rl // 4) % 4 * 32 + b * LEAF_SLOTS + leaf_slot, -1))
        es[:, cols] = onehot(sub[:128] == jnp.where(row // 64 == x, (row // 4) % 16 * 8 + b * 4 + row % 4, -1))

    def take(out, into, send, recv):
        into[z] = out[z]
        for o in Z_NEAR:
            i = (z - o) % NZ
            c = remote(out.at[i], into.at[i], send.at[i], recv.at[i], pos, head)
            c.wait_send()
            c.wait_recv()

    take(sl, rl_in, l_zs, l_zr)
    got = [rl_in[i].astype(F32) for i in range(16)]

    def collect(first, rows):
        v = jnp.zeros((rows, 128), F32)
        for i in range(16):
            v = jnp.where(lane // 8 == i, turn(got[i][:rows], 8 * i - first), v)
        return v

    left = jnp.concatenate([collect(0, 16), collect(8, 16), collect(16, 8)], axis=0).astype(BF16)
    from_suffix = dot(left, es[...])

    take(sb, rb, b_zs, b_zr)
    scatter = onehot((iota((128, 128), 0) >= 120) & (iota((128, 128), 0) - 120 == iota((128, 128), 1) % 8))
    stats = dot(rb[...].reshape(512, 128), scatter)
    gap = jnp.zeros((6, 128), F32)
    got = []
    for i in range(16):
        high = jnp.sum(jnp.where(spread, stats[i * 32:i * 32 + 16], 0.0), axis=0, keepdims=True)
        low = jnp.sum(jnp.where(spread, stats[i * 32 + 16:i * 32 + 32], 0.0), axis=0, keepdims=True)
        got.append(jnp.concatenate([rb[i].astype(F32), high, low, gap], axis=0))
    left, leaves = [], []
    for j in range(4):
        left.append(jnp.concatenate([got[4 * k + j] for k in range(4)], axis=1))
        v = turn(got[j], 32)
        for k in range(1, 4):
            v = jnp.where(lane // 32 == k, turn(got[4 * k + j], 32 + 32 * k), v)
        leaves.append(v)
    from_leaf = dot(jnp.concatenate(leaves, axis=1).astype(BF16), el[...])
    from_doc = dot(jnp.concatenate(left, axis=0).astype(BF16), ed[...])

    for b in range(2):
        cols = slice(b * ROWS, (b + 1) * ROWS)
        parts = []
        for v, here in [(from_doc[j * 40:(j + 1) * 40, cols], rd // 4 == x) for j in range(4)] + [
                (from_leaf[:, cols], rl // 16 == x), (from_suffix[:, cols], row // 64 == x)]:
            parts.append((v[:32], jnp.where(here, v[32:33] + v[33:34], NEG), jnp.where(here, 1.0, 0.0)))
        accum, top, total = merged(parts)
        for half in range(2):
            xs[b * 2 + half] = jnp.concatenate(
                [accum[half * 16:half * 16 + 16], top, total, jnp.zeros((6, ROWS), F32)], axis=0)

    for o in (2, 1, 3):
        push(xs.at[(x + o) % NX], xr.at[x], b_xs.at[o], b_xr.at[o], at_xz(x + o, z), head)
    xr[x] = xs[x]
    for o in (1, 3, 2):
        block = xr.at[(x - o) % NX]
        remote(block, block, b_xs.at[o], b_xr.at[o], pos, head).wait_recv()
    parts = []
    for i in range(NX):
        v = xr[i]
        parts.append((v[:16], v[16:17], v[17:18]))
    accum, _, total = merged(parts)

    at[z] = (accum / total).astype(BF16)
    for o in Z_FAR:
        push(at.at[z], at.at[z], c_zs.at[16 - o], c_zr.at[16 - o], at_xz(x, z + o), head)
    for o in (1, 3, 2):
        block = wx.at[(x - o) % NX]
        remote(block, block, w_s.at[o], w_r.at[o], pos, head).wait_recv()
    for r in Z_NEAR:
        block = at.at[(z + r) % NZ]
        remote(block, block, c_zs.at[r], c_zr.at[r], pos, head).wait_recv()

    eye = onehot(iota((ROWS, ROWS), 0) == iota((ROWS, ROWS), 1))
    attention = dot_nt(eye, at[...].reshape(ROWS, ROWS)).astype(BF16)
    for i in (2, 1, 3, 0):
        to = (x + i) % NX
        share = dot(attention, wx[to].reshape(2 * HD, HD)).astype(BF16)
        for n in range(NH):
            ob[to, n] = share[n * 32:(n + 1) * 32]
        for o in (4, 3, 5, 2, 6, 1, 7, 0):
            if i or o:
                n = (head + o) % NH
                push(ob.at[to, n], db.at[x, head], d_s.at[i * 8 + o], d_r.at[i * 8 + o], at_xz(to, z), n)
    db[x, head] = ob[x, head]
    for i in (1, 3, 2, 0):
        for o in range(NH):
            if i or o:
                block = db.at[(x - i) % NX, (head - o) % NH]
                remote(block, block, d_s.at[i * 8 + o], d_r.at[i * 8 + o], pos, head).wait_recv()
    out_ref[...] = jnp.sum(db[...].reshape(NX * NH, 32, HD).astype(F32), axis=0).astype(BF16)
    for c in sends:
        c.wait_send()


def per_device(queries, doc_kv, leaf_kv, suffix_kv, suffix_len, parent, row_leaf, out_weight):
    vmem = pl.BlockSpec(memory_space=pltpu.VMEM)
    smem = pl.BlockSpec(memory_space=pltpu.SMEM)
    hbm = pl.BlockSpec(memory_space=pl.ANY)
    dma = pltpu.SemaphoreType.DMA
    return pl.pallas_call(
        kernel,
        out_shape=jax.ShapeDtypeStruct((32, 128), BF16),
        in_specs=[hbm, smem, hbm, hbm, hbm, hbm, hbm, hbm],
        out_specs=vmem,
        scratch_shapes=[
            pltpu.VMEM((4, 1024), BF16),
            pltpu.VMEM((1, 64), I32),
            pltpu.VMEM((1, 256), I32),
            pltpu.VMEM((2, 2048, HD), BF16),
            pltpu.VMEM((2, 1024, HD), BF16),
            pltpu.VMEM((2, 4, 512, HD), BF16),
            pltpu.VMEM((4, 2, 4, 2, 16, HD), BF16),
            pltpu.VMEM((HD, 2048), BF16),
            pltpu.VMEM((HD, 1024), BF16),
            pltpu.VMEM((HD, 2048), BF16),
            pltpu.VMEM((NX, 4, 4, 16, HD), BF16),
            pltpu.VMEM((64, 32, HD), BF16),
            pltpu.VMEM((NX, 256, 256), BF16),
            pltpu.VMEM((512, 512), BF16),
            pltpu.VMEM((512, 512), BF16),
            pltpu.VMEM((128, 512), BF16),
            pltpu.VMEM((16, 16, 128), BF16),
            pltpu.VMEM((16, 16, 128), BF16),
            pltpu.VMEM((16, 32, 128), BF16),
            pltpu.VMEM((16, 32, 128), BF16),
            pltpu.VMEM((4, 24, ROWS), F32),
            pltpu.VMEM((4, 24, ROWS), F32),
            pltpu.VMEM((16, 16, ROWS), BF16),
            pltpu.VMEM((NX, NH, 32, HD), BF16),
            pltpu.VMEM((NX, NH, 32, HD), BF16),
            dma((7,)),
            dma((16,)), dma((16,)), dma((64,)), dma((64,)),
            dma((16,)), dma((16,)),
            dma((16,)), dma((16,)), dma((4,)), dma((4,)),
            dma((16,)), dma((16,)), dma((4,)), dma((4,)),
            dma((32,)), dma((32,)),
        ],
        compiler_params=pltpu.CompilerParams(
            collective_id=0, has_side_effects=True, vmem_limit_bytes=62 << 20),
        name="tree_attention",
    )(queries, suffix_len, parent.reshape(1, -1), row_leaf.reshape(1, -1), doc_kv, leaf_kv, suffix_kv,
      out_weight.reshape(4, 2, 4, 2, 16, HD))


def solution(mesh):
    in_specs = (
        P("seq", "head"),
        P(None, "seq", "head"),
        P(None, "seq", "head"),
        P(None, "seq", None, "head"),
        P("seq"),
        P(),
        P(),
        P("head", "seq"),
    )
    return jax.shard_map(
        per_device, mesh=mesh, in_specs=in_specs, out_specs=P("head", "seq"), check_vma=False)
```

time: 66.4 us -> 64 us (0.964)
  Pallas kernels: 64.9 us -> 62.5 us
    pallas_call x1, Pallas kernels: 64.9 us -> 62.5 us  [per_device(): pl.pallas_call(kernel, out_shape=jax.ShapeDtypeStruct((32, 128), BF16), i...]
where the time goes in v3:
time: 64 us; the launch traced here: 63.8 us
  Pallas kernels  62.5 us (98%)
  local copies, waits for them, and re-layouts  1.3 us (2%)
    pallas_call x1, Pallas kernels, per_device(): pl.pallas_call(kernel, out_shape=jax.ShapeDtypeStruct((32, 128), BF16), i...  62.5 us
    unnamed x1, local copies, waits for them, and re-layouts  1.3 us

profile of v3, /device:TPU:1, one launch (start us, length us, event | category | flops | bytes accessed | tf_op | source)
XLA Modules:
  0.0 63.8 jit_solution(8924364827650442619)
XLA Ops:
  0.0 62.5 %tree_attention.1 = bf16[32,128]{1,0:T(8,128)(2,1)} custom-call(bf16[4,1024]{1,0:T(4,128)(2,1)} %q_hbm.1, s32[4]{0:T(128)} %len_ref.1, s32[1,64]{1,0:T(1,128)} %bitcast.5, s32[1,256]{1,0:T(1,128)} %bitcast.4, bf16[2,2048,128]{2,1,0:T(8,128)(2,1)} %doc_hbm.1, bf16[2,1024,128]{2,1,0:T(8,128)(2,1)} %leaf_hbm.1, bf16[2,4,512,128]{3,2,1,0:T(8,128)(2,1)} %suf_hbm.1, ...), custom_call_target="tpu_custom_call" | custom-call | tf_op jit(solution)/shard_map/tree_attention/pallas_call | solution.py:355
  62.5 1.3 %copy.10 = bf16[32,128]{1,0:T(8,128)(2,1)} copy(bf16[32,128]{1,0:T(8,128)(2,1)} %tree_attention.1) | data formatting | bytes 16384

commit v4 on v3

--- a/solution.py
+++ b/solution.py
@@ -21,7 +21,7 @@
 NT = (((1,), (1,)), ((), ()))
 Z_FAR = (8, 7, 9, 6, 10, 5, 11, 4, 12, 3, 13, 2, 14, 1, 15)
 Z_NEAR = Z_FAR[::-1]
-Z_STEP = (4, 12, 3, 13, 2, 14, 1, 15)
+Z_STEP = (1, 15, 2, 14, 3, 13, 4, 12)
 
 
 def iota(shape, dim):
@@ -144,6 +144,11 @@
         c.start()
         sends.append(c)
 
+    def sent():
+        for c in sends:
+            c.wait_send()
+        sends.clear()
+
     for o in Z_STEP:
         push(qa.at[pos], qa.at[pos], a_zs.at[16 - o], a_zr.at[16 - o], at_xz(x, z + o), head)
     for r in (0, 1, 15, 2, 14, 3, 13, 4, 12, 5, 11, 6, 10, 7, 9, 8):
@@ -154,7 +159,7 @@
             push(block, block, a_zs.at[r + 4], a_zr.at[r + 4], at_xz(x, z - 4), head)
         if 13 <= r <= 15:
             push(block, block, a_zs.at[r - 4], a_zr.at[r - 4], at_xz(x, z + 4), head)
-        for i in (2, 1, 3):
+        for i in (1, 3, 2):
             push(block, block, a_xs.at[i * 16 + r], a_xr.at[i * 16 + r], at_xz(x + i, z), head)
 
     loads[0].wait()
@@ -239,6 +244,8 @@
             sb[pair * 4 + c] = jnp.where(lane < 120, accum[c * 32:(c + 1) * 32], both).astype(BF16)
         send_parts(sb, rb, b_zs, b_zr, pair)
 
+    sent()
+
     loads[3].wait()
     for o in (2, 1, 3):
         to = (x + o) % NX
@@ -316,8 +323,12 @@
     accum, _, total = merged(parts)
 
     at[z] = (accum / total).astype(BF16)
+    before_z = list(sends)
+    sends.clear()
     for o in Z_FAR:
         push(at.at[z], at.at[z], c_zs.at[16 - o], c_zr.at[16 - o], at_xz(x, z + o), head)
+    for c in before_z:
+        c.wait_send()
     for o in (1, 3, 2):
         block = wx.at[(x - o) % NX]
         remote(block, block, w_s.at[o], w_r.at[o], pos, head).wait_recv()
@@ -337,14 +348,13 @@
                 n = (head + o) % NH
                 push(ob.at[to, n], db.at[x, head], d_s.at[i * 8 + o], d_r.at[i * 8 + o], at_xz(to, z), n)
     db[x, head] = ob[x, head]
+    sent()
     for i in (1, 3, 2, 0):
         for o in range(NH):
             if i or o:
                 block = db.at[(x - i) % NX, (head - o) % NH]
                 remote(block, block, d_s.at[i * 8 + o], d_r.at[i * 8 + o], pos, head).wait_recv()
     out_ref[...] = jnp.sum(db[...].reshape(NX * NH, 32, HD).astype(F32), axis=0).astype(BF16)
-    for c in sends:
-        c.wait_send()
 
 
 def per_device(queries, doc_kv, leaf_kv, suffix_kv, suffix_len, parent, row_leaf, out_weight):

time: 64 us -> 63.5 us (level)
  no operation moved by 1% of the time
where the time goes in v4:
time: 63.5 us; the launch traced here: 63.3 us
  Pallas kernels  62 us (98%)
  local copies, waits for them, and re-layouts  1.3 us (2%)
    pallas_call x1, Pallas kernels, per_device(): pl.pallas_call(kernel, out_shape=jax.ShapeDtypeStruct((32, 128), BF16), i...  62 us
    unnamed x1, local copies, waits for them, and re-layouts  1.3 us

profile of v4, /device:TPU:1, one launch (start us, length us, event | category | flops | bytes accessed | tf_op | source)
XLA Modules:
  0.0 63.3 jit_solution(15153704839321161550)
XLA Ops:
  0.0 62.0 %tree_attention.1 = bf16[32,128]{1,0:T(8,128)(2,1)} custom-call(bf16[4,1024]{1,0:T(4,128)(2,1)} %q_hbm.1, s32[4]{0:T(128)} %len_ref.1, s32[1,64]{1,0:T(1,128)} %bitcast.5, s32[1,256]{1,0:T(1,128)} %bitcast.4, bf16[2,2048,128]{2,1,0:T(8,128)(2,1)} %doc_hbm.1, bf16[2,1024,128]{2,1,0:T(8,128)(2,1)} %leaf_hbm.1, bf16[2,4,512,128]{3,2,1,0:T(8,128)(2,1)} %suf_hbm.1, ...), custom_call_target="tpu_custom_call" | custom-call | tf_op jit(solution)/shard_map/tree_attention/pallas_call | solution.py:365
  62.0 1.3 %copy.10 = bf16[32,128]{1,0:T(8,128)(2,1)} copy(bf16[32,128]{1,0:T(8,128)(2,1)} %tree_attention.1) | data formatting | bytes 16384
